TPU v7x, 32 devices: a whole 2x2x4 slice. The times are simulated.
32 devices in a mesh: groups: 2 (over x), seq: 8 (over z, y), head: 2 (over core).
Axes of the slice: x: 2, y: 2, z: 4, core: 2. Of those that a mesh axis runs over, the one named last changes fastest.
Arguments:
- query_proj: bfloat16 [3072, 2048], P(('groups', 'seq'), 'head'), parts along dimension 0, may hold values from -43 to 43
- key_proj: bfloat16 [3072, 2048], P(('groups', 'seq'), 'head'), parts along dimension 0, may hold values from -43 to 43
- value_proj: bfloat16 [3072, 4096], P(('groups', 'seq'), 'head'), parts along dimension 0, may hold values from -43 to 43
- gate_proj: bfloat16 [3072, 4096], P(('groups', 'seq'), 'head'), parts along dimension 0, may hold values from -6 to 6
- write_strength: float32 [3072, 32], P(('groups', 'seq'), 'head'), parts along dimension 0, may hold values from 0 to 1
- log_decay: float32 [3072, 32], P(('groups', 'seq'), 'head'), parts along dimension 0, may hold values from -2 to 0
- conv_query: bfloat16 [4, 2048], P(None, 'head'), may hold values from -3 to 3
- conv_key: bfloat16 [4, 2048], P(None, 'head'), may hold values from -3 to 3
- conv_value: bfloat16 [4, 4096], P(None, 'head'), may hold values from -3 to 3
- norm_gain: float32 [128], replicated, may hold values from 0.5 to 1.5
Outputs:
- mixer_out: bfloat16 [3072, 4096], P(('groups', 'seq'), 'head'), parts along dimension 0
There are 2 independent parts, one for each index of `groups`. A program takes and returns all parts, laid end to end along the dimension named above; an argument that names none is the same for every part. Nothing has to cross between parts.
All inputs are finite; a program needn't handle non-finite values.
Results may differ from a plain program's by a relative error of at most 0.0075.
Values may be sent and summed in bfloat16 or wider, within the bound.
A program may use at most 128 MiB of HBM per device.

v0:
```python
import functools

import jax
import jax.numpy as jnp
from jax import lax
from jax.experimental import pallas as pl
from jax.experimental.pallas import tpu as pltpu
from jax.sharding import PartitionSpec as P

DK = 128
RIM = 8
SOLVE_PASSES = 1
F32 = jnp.float32
BF16 = jnp.bfloat16
NN = (((1,), (0,)), ((), ()))
NT = (((1,), (1,)), ((), ()))
TN = (((0,), (0,)), ((), ()))


def pieces(x):
    high = x.astype(BF16)
    return high, (x - high.astype(F32)).astype(BF16)


def dot(a, b, dims=NN):
    return lax.dot_general(a, b, dims, preferred_element_type=F32)


def dot3(a, b, dims=NN):
    ah, al = pieces(a)
    bh, bl = pieces(b)
    return dot(ah, bh, dims) + dot(ah, bl, dims) + dot(al, bh, dims)


def dot1(a, b, dims=NN):
    return dot(a.astype(BF16), b.astype(BF16), dims)


def silu(u):
    return u / (1.0 + jnp.exp(-u))


def conv_silu(rows, rim_ref, source_ref, taps_ref):
    margin = rim_ref.shape[0]
    count = source_ref.shape[0]
    rows[RIM - margin : RIM, :] = rim_ref[...].astype(F32)
    rows[RIM : RIM + count, :] = source_ref[...].astype(F32)
    taps = taps_ref[...].astype(F32)
    total = taps[0:1] * rows[RIM - margin : RIM - margin + count, :]
    for j in range(1, taps.shape[0]):
        total = total + taps[j : j + 1] * rows[RIM - margin + j : RIM - margin + j + count, :]
    return silu(total).astype(BF16).astype(F32)


def unit(x):
    return x * lax.rsqrt(jnp.sum(x * x, axis=-1, keepdims=True) + 1e-06)


def local_kernel(
    ratio,
    rim_q, rim_k, rim_v, q_ref, k_ref, v_ref, beta_ref, decay_ref, tq, tk, tv,
    map_high, map_low, base_ref,
    rows_q, rows_k, rows_v, cum_ref, cum_t_ref,
):
    step = pl.program_id(0)
    count = q_ref.shape[0]
    row = lax.broadcasted_iota(jnp.int32, (count, count), 0)
    column = lax.broadcasted_iota(jnp.int32, (count, count), 1)
    upto = row >= column
    apart = jnp.where(upto, row ^ column, 0)

    @pl.when(step == 0)
    def _():
        ones = upto.astype(F32)
        cum_ref[...] = lax.dot_general(
            ones, decay_ref[...], NN, precision=lax.Precision.HIGHEST, preferred_element_type=F32
        )
        cum_t_ref[...] = lax.dot_general(
            decay_ref[...], ones, (((0,), (1,)), ((), ())),
            precision=lax.Precision.HIGHEST, preferred_element_type=F32,
        )

    query = unit(conv_silu(rows_q, rim_q, q_ref, tq)) * (DK ** -0.5)
    key = unit(conv_silu(rows_k, rim_k, k_ref, tk))
    value = conv_silu(rows_v, rim_v, v_ref, tv)
    gram = dot3(key, key, NT)
    scores = dot3(query, key, NT)
    heads = range(ratio)
    lane = lax.broadcasted_iota(jnp.int32, beta_ref.shape, 1)
    cum, beta, fade, lower = [], [], [], []
    for r in heads:
        head = step * ratio + r
        chosen = lane == head
        c = jnp.sum(jnp.where(chosen, cum_ref[...], 0.0), axis=1, keepdims=True)
        b = jnp.sum(jnp.where(chosen, beta_ref[...], 0.0), axis=1, keepdims=True)
        gap = c - cum_t_ref[pl.ds(head, 1), :]
        f = jnp.where(upto, jnp.exp(jnp.where(upto, gap, 0.0)), 0.0)
        cum.append(c)
        beta.append(b)
        fade.append(f)
        lower.append(b * gram * f)
    identity = (row == column).astype(F32)
    first = apart == 1
    inverse = [identity - jnp.where(first, lower[r], 0.0) for r in heads]
    multiply = dot1 if SOLVE_PASSES == 1 else dot3
    width = 2
    while width < count:
        mask = (apart >= width) & (apart < 2 * width)
        inner = [multiply(jnp.where(mask, lower[r], 0.0), inverse[r]) for r in heads]
        inverse = [inverse[r] - multiply(inverse[r], inner[r]) for r in heads]
        width *= 2
    small = identity[:DK, :DK]
    for r in heads:
        grown = jnp.exp(cum[r])
        right = jnp.concatenate(
            [beta[r] * value[:, r * DK : (r + 1) * DK], (beta[r] * grown) * key], axis=1
        )
        solved = dot3(inverse[r], right)
        last = cum[r][count - 1 : count, :]
        ahead = dot3(key * jnp.exp(last - cum[r]), solved, TN)
        out = dot3(scores * fade[r], solved)
        base_ref[r, 0:DK, :] = ahead[:, :DK]
        base_ref[r, DK : DK + count, :] = out[:, :DK]
        mh, ml = pieces(jnp.exp(last) * small - ahead[:, DK:])
        map_high[r, 0:DK, :] = mh
        map_low[r, 0:DK, :] = ml
        qh, ql = pieces(grown * query - out[:, DK:])
        map_high[r, DK : DK + count, :] = qh
        map_low[r, DK : DK + count, :] = ql


def local_part(rim, query_proj, key_proj, value_proj, beta, decay, conv_q, conv_k, conv_v):
    count = query_proj.shape[0]
    key_heads = query_proj.shape[1] // DK
    heads = beta.shape[1]
    ratio = heads // key_heads
    margin = rim.shape[0]
    width = conv_q.shape[0]
    vw = ratio * DK
    v_first = 2 * key_heads // ratio

    def col(height, w, first=0):
        return pl.BlockSpec((height, w), lambda i: (0, first + i))

    whole = pl.BlockSpec((count, heads), lambda i: (0, 0))
    tall = DK + count
    spec = pl.BlockSpec((ratio, tall, DK), lambda i: (i, 0, 0))
    shape = (heads, tall, DK)
    return pl.pallas_call(
        functools.partial(local_kernel, ratio),
        grid=(key_heads,),
        in_specs=[
            col(margin, DK), col(margin, DK, key_heads), col(margin, vw, v_first),
            col(count, DK), col(count, DK), col(count, vw), whole, whole,
            col(width, DK), col(width, DK), col(width, vw),
        ],
        out_specs=[spec, spec, spec],
        out_shape=[
            jax.ShapeDtypeStruct(shape, BF16),
            jax.ShapeDtypeStruct(shape, BF16),
            jax.ShapeDtypeStruct(shape, F32),
        ],
        scratch_shapes=[
            pltpu.VMEM((RIM + count, DK), F32),
            pltpu.VMEM((RIM + count, DK), F32),
            pltpu.VMEM((RIM + count, vw), F32),
            pltpu.VMEM((count, heads), F32),
            pltpu.VMEM((heads, count), F32),
        ],
        compiler_params=pltpu.CompilerParams(vmem_limit_bytes=40 * 2**20),
        name="local_blocks",
    )(rim, rim, rim, query_proj, key_proj, value_proj, beta, decay, conv_q, conv_k, conv_v)


def relay_kernel(
    n, map_high, map_low, base_ref, gate_ref, gain_ref, out_ref, entering, leaving, send_sem, recv_sem
):
    me = lax.axis_index("seq")
    heads = map_high.shape[0]
    has_left = me > 0
    has_right = me < n - 1
    left = lax.rem(me + n - 1, n)
    right = lax.rem(me + 1, n)
    barrier = pltpu.get_barrier_semaphore()

    @pl.when(has_left)
    def _():
        pl.semaphore_signal(
            barrier, inc=1, device_id={"seq": left}, device_id_type=pl.DeviceIdType.MESH
        )

    @pl.when(has_right)
    def _():
        pl.semaphore_wait(barrier, 1)

    def hop(h):
        return pltpu.make_async_remote_copy(
            src_ref=leaving.at[h],
            dst_ref=entering.at[h],
            send_sem=send_sem.at[h],
            recv_sem=recv_sem.at[h],
            device_id={"seq": right},
            device_id_type=pl.DeviceIdType.MESH,
        )

    @pl.when(jnp.logical_not(has_left))
    def _():
        entering[...] = jnp.zeros_like(entering)

    gain = gain_ref[...]
    for h in range(heads):
        @pl.when(has_left)
        def _():
            hop(h).wait_recv()

        state = entering[h]

        @pl.when(has_right)
        def _():
            ahead = dot(map_high[h, :DK], state) + dot(map_low[h, :DK], state) + base_ref[h, :DK]
            leaving[h] = ahead.astype(leaving.dtype)
            hop(h).start()

        rows = dot(map_high[h, DK:], state) + dot(map_low[h, DK:], state) + base_ref[h, DK:]
        mean = jnp.mean(rows * rows, axis=-1, keepdims=True)
        gate = gate_ref[:, h * DK : (h + 1) * DK].astype(F32)
        out = rows * lax.rsqrt(mean + 1e-06) * gain * silu(gate)
        out_ref[:, h * DK : (h + 1) * DK] = out.astype(BF16)

    @pl.when(has_right)
    def _():
        for h in range(heads):
            hop(h).wait_send()


def relay_part(n, map_high, map_low, base, gate, gain):
    heads = map_high.shape[0]
    vmem = pl.BlockSpec(memory_space=pltpu.VMEM)
    return pl.pallas_call(
        functools.partial(relay_kernel, n),
        in_specs=[vmem] * 5,
        out_specs=vmem,
        out_shape=jax.ShapeDtypeStruct(gate.shape, BF16),
        scratch_shapes=[
            pltpu.VMEM((heads, DK, DK), BF16),
            pltpu.VMEM((heads, DK, DK), BF16),
            pltpu.SemaphoreType.DMA((heads,)),
            pltpu.SemaphoreType.DMA((heads,)),
        ],
        compiler_params=pltpu.CompilerParams(
            collective_id=0, has_side_effects=True, vmem_limit_bytes=40 * 2**20
        ),
        name="relay",
    )(map_high, map_low, base, gate, gain.reshape(1, -1))


def shards(
    query_proj, key_proj, value_proj, gate_proj, write_strength, log_decay,
    conv_query, conv_key, conv_value, norm_gain,
):
    n = lax.axis_size("seq")
    margin = conv_query.shape[0] - 1
    tails = jnp.concatenate(
        [query_proj[-margin:], key_proj[-margin:], value_proj[-margin:]], axis=1
    )
    rim = lax.ppermute(tails, "seq", [(i, i + 1) for i in range(n - 1)])
    parts = local_part(
        rim, query_proj, key_proj, value_proj, write_strength, log_decay,
        conv_query, conv_key, conv_value,
    )
    return relay_part(n, *parts, gate_proj, norm_gain)


def solution(mesh):
    split = P(("groups", "seq"), "head")
    in_specs = (split,) * 6 + (P(None, "head"),) * 3 + (P(),)
    return jax.shard_map(shards, mesh=mesh, in_specs=in_specs, out_specs=split, check_vma=False)
```

profile of v0, /device:TPU:28, one launch (start us, length us, event | category | flops | bytes accessed | tf_op | source)
XLA Modules:
  0.0 77.2 jit_solution(10346224614962316189)
XLA Ops:
  0.0 0.0 copy-start.7
  0.0 0.7 slice.9
  0.7 0.7 slice.10
  1.5 0.8 slice.11
  2.3 1.3 %collective-permute-start = (bf16[3,4096]{1,0:T(4,128)(2,1)S(1)}, bf16[3,4096]{1,0:T(4,128)(2,1)S(1)}, u32[]{:S(2)}, u32[]{:S(2)}) collective-permute-start(bf16[3,4096]{1,0:T(4,128)(2,1)S(1)} %pad_maximum_fusion), channel_id=1, source_target_pairs={{0,2},{2,4},{4,6},{6,8},{8,10},{10,12},{12,14},{1,3},{3,5},{5,7},{... | collective-permute-start | bytes 73736 | tf_op jit(solution)/shard_map/ppermute | solution.py:266
  3.6 0.8 %copy.11.beta_ref = f32[192,16]{1,0:T(8,128)S(1)} copy(f32[192,16]{0,1:T(8,128)} %param.14) | data formatting | bytes 24576 | tf_op args[4]
  4.4 0.8 %copy.12.decay_ref = f32[192,16]{1,0:T(8,128)S(1)} copy(f32[192,16]{0,1:T(8,128)} %param.15) | data formatting | bytes 24576 | tf_op args[5]
  5.2 2.9 %collective-permute-done.rim_q.rim_k.rim_v = bf16[3,4096]{1,0:T(4,128)(2,1)S(1)} collective-permute-done((bf16[3,4096]{1,0:T(4,128)(2,1)S(1)}, bf16[3,4096]{1,0:T(4,128)(2,1)S(1)}, u32[]{:S(2)}, u32[]{:S(2)}) %collective-permute-start) | collective-permute-done | bytes 24608 | tf_op jit(solution)/shard_map/ppermute | solution.py:266
  8.1 0.0 copy-start
  8.1 1.1 %copy-done = bf16[192,2048]{1,0:T(8,128)(2,1)S(1)} copy-done((bf16[192,2048]{1,0:T(8,128)(2,1)S(1)}, bf16[192,2048]{1,0:T(8,128)(2,1)}, u32[]{:S(2)}) %copy-start) | copy-done | bytes 786456
  9.2 0.0 copy-start.2
  9.2 1.0 %copy-done.2 = bf16[192,1024]{1,0:T(8,128)(2,1)S(1)} copy-done((bf16[192,1024]{1,0:T(8,128)(2,1)S(1)}, bf16[192,1024]{1,0:T(8,128)(2,1)}, u32[]{:S(2)}) %copy-start.2) | copy-done | bytes 393240
  10.2 0.0 copy-start.3
  10.2 1.0 %copy-done.3 = bf16[192,1024]{1,0:T(8,128)(2,1)S(1)} copy-done((bf16[192,1024]{1,0:T(8,128)(2,1)S(1)}, bf16[192,1024]{1,0:T(8,128)(2,1)}, u32[]{:S(2)}) %copy-start.3) | copy-done | bytes 393240
  11.2 0.0 copy-start.4
  11.2 0.7 copy-done.4
  11.9 0.0 copy-start.5
  11.9 0.7 copy-done.5
  12.6 0.0 copy-start.6
  12.6 0.7 copy-done.6
  13.3 0.0 copy-start.1
  13.3 30.8 %local_blocks.1 = (bf16[16,320,128]{2,1,0:T(8,128)(2,1)S(1)}, bf16[16,320,128]{2,1,0:T(8,128)(2,1)S(1)}, f32[16,320,128]{2,1,0:T(8,128)S(1)}) custom-call(bf16[3,4096]{1,0:T(4,128)(2,1)S(1)} %collective-permute-done.rim_q.rim_k.rim_v, bf16[3,4096]{1,0:T(4,128)(2,1)S(1)} %collective-permute-done.rim_q.rim_k.rim_v, ...), custom_call_target="tpu_custom_call" | custom-call | tf_op jit(solution)/shard_map/local_blocks/pallas_call | solution.py:149
  44.1 0.0 copy-done.7
  44.1 0.0 copy-done.1
  44.1 32.2 %relay.1 = bf16[192,2048]{1,0:T(8,128)(2,1)S(1)} custom-call(bf16[16,320,128]{2,1,0:T(8,128)(2,1)S(1)} %get-tuple-element.8.map_high, bf16[16,320,128]{2,1,0:T(8,128)(2,1)S(1)} %get-tuple-element.9.map_low, f32[16,320,128]{2,1,0:T(8,128)S(1)} %get-tuple-element.10.base_ref, bf16[192,2048]{1,0:T(8,128)(2,1)S(1)} %copy-done.1, f32[1,128]{1,0:T(1,128)S(1)} %bitcast.1), custom_call_target="tpu_custom_call" | custom-call | tf_op jit(solution)/shard_map/relay/pallas_call | solution.py:239
  76.3 0.9 %copy.14 = bf16[192,2048]{1,0:T(8,128)(2,1)} copy(bf16[192,2048]{1,0:T(8,128)(2,1)S(1)} %relay.1) | data formatting | bytes 1572864
  (1 shorter events, 0.0 us)
Async XLA Ops:
  0.0 44.1 %copy-start.7 = (f32[128]{0:T(128)S(1)}, f32[128]{0:T(128)}, u32[]{:S(2)}) copy-start(f32[128]{0:T(128)} %param.19) | copy-start | bytes 1540
  2.3 5.8 %collective-permute-start = (bf16[3,4096]{1,0:T(4,128)(2,1)S(1)}, bf16[3,4096]{1,0:T(4,128)(2,1)S(1)}, u32[]{:S(2)}, u32[]{:S(2)}) collective-permute-start(bf16[3,4096]{1,0:T(4,128)(2,1)S(1)} %pad_maximum_fusion), channel_id=1, source_target_pairs={{0,2},{2,4},{4,6},{6,8},{8,10},{10,12},{12,14},{1,3},{3,5},{5,7},{... | collective-permute-start | bytes 73736 | tf_op jit(solution)/shard_map/ppermute | solution.py:266
  8.1 1.1 %copy-start = (bf16[192,2048]{1,0:T(8,128)(2,1)S(1)}, bf16[192,2048]{1,0:T(8,128)(2,1)}, u32[]{:S(2)}) copy-start(bf16[192,2048]{1,0:T(8,128)(2,1)} %v_ref.1) | copy-start | bytes 2359300
  9.2 1.0 %copy-start.2 = (bf16[192,1024]{1,0:T(8,128)(2,1)S(1)}, bf16[192,1024]{1,0:T(8,128)(2,1)}, u32[]{:S(2)}) copy-start(bf16[192,1024]{1,0:T(8,128)(2,1)} %k_ref.1) | copy-start | bytes 1179652
  10.2 1.0 %copy-start.3 = (bf16[192,1024]{1,0:T(8,128)(2,1)S(1)}, bf16[192,1024]{1,0:T(8,128)(2,1)}, u32[]{:S(2)}) copy-start(bf16[192,1024]{1,0:T(8,128)(2,1)} %q_ref.1) | copy-start | bytes 1179652
  11.2 0.7 copy-start.4
  11.9 0.7 copy-start.5
  12.6 0.7 copy-start.6
  13.3 30.8 %copy-start.1 = (bf16[192,2048]{1,0:T(8,128)(2,1)S(1)}, bf16[192,2048]{1,0:T(8,128)(2,1)}, u32[]{:S(2)}) copy-start(bf16[192,2048]{1,0:T(8,128)(2,1)} %gate_ref.1) | copy-start | bytes 2359300
where the time goes:
time: 78 us; the launch traced here: 77.2 us
  Pallas kernels  63 us (81%)
  local copies, waits for them, and re-layouts  9.99 us (13%)
  waiting for transfers between devices  2.87 us (4%)
  starting transfers between devices  1.29 us (2%)
    pallas_call x1, Pallas kernels, relay_part(): pl.pallas_call(functools.partial(relay_kernel, n), in_specs=[vmem] * 5, o...  32.2 us
    pallas_call x1, Pallas kernels, local_part(): pl.pallas_call(functools.partial(local_kernel, ratio), grid=(key_heads,),...  30.8 us
    unnamed x19, local copies, waits for them, and re-layouts  7.76 us
    ppermute x1, waiting for transfers between devices, shards(): rim = lax.ppermute(tails, 'seq', [(i, i + 1) for i in range(n - 1)])  2.87 us
  transfers between devices with their start and end apart: 1, of which 1 were waited for; matrix products, arithmetic and copies ran while one was open for 2% of the time, Pallas kernels for 0%

commit v1 on v0

v1 whole, which is shorter than its diff:
```python
import functools

import jax
import jax.numpy as jnp
from jax import lax
from jax.experimental import pallas as pl
from jax.experimental.pallas import tpu as pltpu
from jax.sharding import PartitionSpec as P

DK = 128
TILE = 16
KEY_HEADS_A_STEP = 2
F32 = jnp.float32
BF16 = jnp.bfloat16
NN = (((1,), (0,)), ((), ()))
NT = (((1,), (1,)), ((), ()))
TN = (((0,), (0,)), ((), ()))


def pieces(x):
    high = x.astype(BF16)
    return high, (x - high.astype(F32)).astype(BF16)


def dot(a, b, dims=NN):
    return lax.dot_general(a, b, dims, preferred_element_type=F32)


def dot3(a, b, dims=NN):
    ah, al = pieces(a)
    bh, bl = pieces(b)
    return dot(ah, bh, dims) + dot(ah, bl, dims) + dot(al, bh, dims)


def dot1(a, b, dims=NN):
    return dot(a.astype(BF16), b.astype(BF16), dims)


def silu(u):
    return u / (1.0 + jnp.exp(-u))


def dot2(a, b, dims=NN):
    bh, bl = pieces(b)
    a = a.astype(BF16)
    return dot(a, bh, dims) + dot(a, bl, dims)


def precise(a, b, dims):
    return lax.dot_general(
        a, b, dims, precision=lax.Precision.HIGHEST, preferred_element_type=F32
    )


def conv_silu(rows, rim, source_ref, taps_ref):
    count = source_ref.shape[0]
    rows[0:TILE, :] = rim.astype(F32)
    rows[TILE : TILE + count, :] = source_ref[...].astype(F32)
    taps = taps_ref[...].astype(F32)
    first = TILE - taps.shape[0] + 1
    total = taps[0:1] * rows[first : first + count, :]
    for j in range(1, taps.shape[0]):
        total = total + taps[j : j + 1] * rows[first + j : first + j + count, :]
    return silu(total).astype(BF16).astype(F32)


def unit(x):
    return x * lax.rsqrt(jnp.sum(x * x, axis=-1, keepdims=True) + 1e-06)


def kernel(
    n, ratio, per_step, steps,
    tail_q, tail_k, tail_v, q_ref, k_ref, v_ref, beta_t, decay_t, tq, tk, tv, gate_ref, gain_ref,
    out_ref,
    rows_q, rows_k, rows_v, cum_ref, cum_t_ref, beta_ref,
    map_high, map_low, reader, base_ref, rim_q, rim_k, rim_v, entering, leaving,
    send_sem, recv_sem, rim_send, rim_recv,
):
    step = pl.program_id(0)
    me = lax.axis_index("seq")
    has_left = me > 0
    has_right = me < n - 1
    left = lax.rem(me + n - 1, n)
    right = lax.rem(me + 1, n)
    count = q_ref.shape[0]
    group = ratio * per_step
    total_heads = group * steps
    row = lax.broadcasted_iota(jnp.int32, (count, count), 0)
    column = lax.broadcasted_iota(jnp.int32, (count, count), 1)
    upto = row >= column
    apart = jnp.where(upto, row ^ column, 0)
    identity = (row == column).astype(F32)

    def rim_hop(i):
        source, target = ((tail_q, rim_q), (tail_k, rim_k), (tail_v, rim_v))[i]
        return pltpu.make_async_remote_copy(
            src_ref=source, dst_ref=target, send_sem=rim_send.at[i], recv_sem=rim_recv.at[i],
            device_id={"seq": right}, device_id_type=pl.DeviceIdType.MESH,
        )

    def hop(h):
        return pltpu.make_async_remote_copy(
            src_ref=leaving.at[h], dst_ref=entering.at[h],
            send_sem=send_sem.at[h], recv_sem=recv_sem.at[h],
            device_id={"seq": right}, device_id_type=pl.DeviceIdType.MESH,
        )

    @pl.when(step == 0)
    def _():
        barrier = pltpu.get_barrier_semaphore()

        @pl.when(has_left)
        def _():
            pl.semaphore_signal(
                barrier, inc=1, device_id={"seq": left}, device_id_type=pl.DeviceIdType.MESH
            )

        @pl.when(has_right)
        def _():
            pl.semaphore_wait(barrier, 1)
            for i in range(3):
                rim_hop(i).start()

        ones = upto.astype(F32)
        cum_ref[...] = precise(ones, decay_t[...], NT)
        cum_t_ref[...] = precise(decay_t[...], ones, NT)
        beta_ref[...] = precise(identity, beta_t[...], NT)

        @pl.when(jnp.logical_not(has_left))
        def _():
            entering[...] = jnp.zeros_like(entering)
            for ref in (rim_q, rim_k, rim_v):
                ref[...] = jnp.zeros_like(ref)

        @pl.when(has_left)
        def _():
            for i in range(3):
                rim_hop(i).wait_recv()

        @pl.when(has_right)
        def _():
            for i in range(3):
                rim_hop(i).wait_send()

    def rim_of(ref, w):
        return ref[:, pl.ds(pl.multiple_of(step * w, 128), w)]

    kw = per_step * DK
    vw = group * DK
    query_all = conv_silu(rows_q, rim_of(rim_q, kw), q_ref, tq)
    key_all = conv_silu(rows_k, rim_of(rim_k, kw), k_ref, tk)
    value = conv_silu(rows_v, rim_of(rim_v, vw), v_ref, tv)
    queries = [unit(query_all[:, g * DK : (g + 1) * DK]) * (DK ** -0.5) for g in range(per_step)]
    keys = [unit(key_all[:, g * DK : (g + 1) * DK]) for g in range(per_step)]
    grams = [dot3(keys[g], keys[g], NT) for g in range(per_step)]
    scores = [dot3(queries[g], keys[g], NT) for g in range(per_step)]
    heads = range(group)
    lane = lax.broadcasted_iota(jnp.int32, beta_ref.shape, 1)
    cum, beta, fade, lower = [], [], [], []
    for r in heads:
        head = step * group + r
        chosen = lane == head
        c = jnp.sum(jnp.where(chosen, cum_ref[...], 0.0), axis=1, keepdims=True)
        b = jnp.sum(jnp.where(chosen, beta_ref[...], 0.0), axis=1, keepdims=True)
        gap = c - cum_t_ref[pl.ds(head, 1), :]
        f = jnp.where(upto, jnp.exp(jnp.where(upto, gap, 0.0)), 0.0)
        cum.append(c)
        beta.append(b)
        fade.append(f)
        lower.append(b * grams[r // ratio] * f)
    inverse = [identity - jnp.where(apart == 1, lower[r], 0.0) for r in heads]
    width = 2
    while width < count:
        mask = (apart >= width) & (apart < 2 * width)
        low = [inverse[r].astype(BF16) for r in heads]
        inner = [dot(jnp.where(mask, lower[r], 0.0).astype(BF16), low[r]) for r in heads]
        inverse = [inverse[r] - dot(low[r], inner[r].astype(BF16)) for r in heads]
        width *= 2
    small = identity[:DK, :DK]
    grown = [jnp.exp(cum[r]) for r in heads]
    solved = []
    for r in heads:
        rhs = jnp.concatenate(
            [
                beta[r] * value[:, r * DK : (r + 1) * DK],
                (beta[r] * grown[r]) * keys[r // ratio],
            ],
            axis=1,
        )
        solved.append(dot3(inverse[r], rhs))
    for r in heads:
        head = step * group + r
        last = cum[r][count - 1 : count, :]
        faded = keys[r // ratio] * jnp.exp(last - cum[r])
        ahead = dot2(faded, solved[r], TN)
        out = dot1(scores[r // ratio] * fade[r], solved[r])
        base_ref[head, 0:DK, :] = ahead[:, :DK]
        base_ref[head, DK : DK + count, :] = out[:, :DK]
        mh, ml = pieces(jnp.exp(last) * small - ahead[:, DK:])
        map_high[head] = mh
        map_low[head] = ml
        reader[head] = (grown[r] * queries[r // ratio] - out[:, DK:]).astype(BF16)

    def step_state(h):
        state = entering[h]
        new = dot(map_high[h], state) + dot(map_low[h], state) + base_ref[h, 0:DK, :]
        leaving[h] = new.astype(BF16)

    def forward(p):
        @pl.when(has_left)
        def _():
            for r in heads:
                hop(p * group + r).wait_recv()

        @pl.when(has_right)
        def _():
            for r in heads:
                step_state(p * group + r)
            for r in heads:
                hop(p * group + r).start()

    def forward_each(p):
        for r in heads:
            h = p * group + r

            @pl.when(has_left)
            def _():
                hop(h).wait_recv()

            @pl.when(has_right)
            def _():
                step_state(h)
                hop(h).start()

    gain = gain_ref[...]

    def finish(p):
        for r in heads:
            h = p * group + r
            place = pl.ds(pl.multiple_of(h * DK, DK), DK)
            rows = dot(reader[h], entering[h]) + base_ref[h, DK : DK + count, :]
            mean = jnp.mean(rows * rows, axis=-1, keepdims=True)
            gate = gate_ref[:, place].astype(F32)
            out_ref[:, place] = (rows * lax.rsqrt(mean + 1e-06) * gain * silu(gate)).astype(BF16)

    @pl.when(step >= me)
    def _():
        forward(step - me)

    @pl.when(step == steps - 1)
    def _():
        start = jnp.maximum(steps - me, 0)

        @pl.loop(start, steps)
        def _(p):
            forward_each(p)
            finish(p)

        @pl.loop(0, start)
        def _(p):
            finish(p)

        @pl.when(has_right)
        def _():
            for h in range(total_heads):
                hop(h).wait_send()


def shards(
    query_proj, key_proj, value_proj, gate_proj, write_strength, log_decay,
    conv_query, conv_key, conv_value, norm_gain,
):
    n = lax.axis_size("seq")
    count = query_proj.shape[0]
    key_heads = query_proj.shape[1] // DK
    heads = write_strength.shape[1]
    ratio = heads // key_heads
    per_step = KEY_HEADS_A_STEP
    steps = key_heads // per_step
    taps = conv_query.shape[0]
    kw = per_step * DK
    vw = ratio * kw

    def col(height, w):
        return pl.BlockSpec((height, w), lambda i: (0, i))

    def whole(x):
        return pl.BlockSpec(x.shape, lambda i: (0, 0))

    def tail(x):
        return pl.BlockSpec((TILE, x.shape[1]), lambda i: (count // TILE - 1, 0))

    beta_t = write_strength.T
    decay_t = log_decay.T
    gain = norm_gain.reshape(1, -1)
    return pl.pallas_call(
        functools.partial(kernel, n, ratio, per_step, steps),
        grid=(steps,),
        in_specs=[
            tail(query_proj), tail(key_proj), tail(value_proj),
            col(count, kw), col(count, kw), col(count, vw), whole(beta_t), whole(decay_t),
            col(taps, kw), col(taps, kw), col(taps, vw), whole(gate_proj), whole(gain),
        ],
        out_specs=whole(gate_proj),
        out_shape=jax.ShapeDtypeStruct(gate_proj.shape, BF16),
        scratch_shapes=[
            pltpu.VMEM((TILE + count, kw), F32),
            pltpu.VMEM((TILE + count, kw), F32),
            pltpu.VMEM((TILE + count, vw), F32),
            pltpu.VMEM((count, heads), F32),
            pltpu.VMEM((heads, count), F32),
            pltpu.VMEM((count, heads), F32),
            pltpu.VMEM((heads, DK, DK), BF16),
            pltpu.VMEM((heads, DK, DK), BF16),
            pltpu.VMEM((heads, count, DK), BF16),
            pltpu.VMEM((heads, DK + count, DK), F32),
            pltpu.VMEM((TILE, query_proj.shape[1]), BF16),
            pltpu.VMEM((TILE, key_proj.shape[1]), BF16),
            pltpu.VMEM((TILE, value_proj.shape[1]), BF16),
            pltpu.VMEM((heads, DK, DK), BF16),
            pltpu.VMEM((heads, DK, DK), BF16),
            pltpu.SemaphoreType.DMA((heads,)),
            pltpu.SemaphoreType.DMA((heads,)),
            pltpu.SemaphoreType.DMA((3,)),
            pltpu.SemaphoreType.DMA((3,)),
        ],
        compiler_params=pltpu.CompilerParams(
            collective_id=0, has_side_effects=True, vmem_limit_bytes=56 * 2**20
        ),
        name="delta_layer",
    )(
        query_proj, key_proj, value_proj, query_proj, key_proj, value_proj, beta_t, decay_t,
        conv_query, conv_key, conv_value, gate_proj, gain,
    )


def solution(mesh):
    split = P(("groups", "seq"), "head")
    in_specs = (split,) * 6 + (P(None, "head"),) * 3 + (P(),)
    return jax.shard_map(shards, mesh=mesh, in_specs=in_specs, out_specs=split, check_vma=False)
```

time: 78 us -> 51.8 us (0.66)
  Pallas kernels: 63 us -> 49.5 us
  local copies, waits for them, and re-layouts: 9.99 us -> 2.09 us
  waiting for transfers between devices: 2.87 us -> 0 us
  starting transfers between devices: 1.29 us -> 0 us
    pallas_call x2 -> x1, Pallas kernels: 63 us -> 49.5 us  [shards(): pl.pallas_call(functools.partial(kernel, n, ratio, per_step, steps), grid...]
    unnamed x19 -> x1, local copies, waits for them, and re-layouts: 7.76 us -> 2.09 us
    ppermute x1 -> x0, waiting for transfers between devices: 2.87 us -> none  [shards(): rim = lax.ppermute(tails, 'seq', [(i, i + 1) for i in range(n - 1)])]
    slice x3 -> x0, local copies, waits for them, and re-layouts: 2.23 us -> none  [the longest x1 0.77 us: shards(): value_proj[-margin:]]
    ppermute x1 -> x0, starting transfers between devices: 1.29 us -> none  [shards(): rim = lax.ppermute(tails, 'seq', [(i, i + 1) for i in range(n - 1)])]
  transfers between devices with their start and end apart: 1 -> 0, of which waited for: 1 -> 0; matrix products, arithmetic and copies ran while one was open for 2% -> 0% of each run, Pallas kernels for 0% -> 0%
where the time goes in v1:
time: 51.8 us; the launch traced here: 51.6 us
  Pallas kernels  49.5 us (96%)
  local copies, waits for them, and re-layouts  2.09 us (4%)
    pallas_call x1, Pallas kernels, shards(): pl.pallas_call(functools.partial(kernel, n, ratio, per_step, steps), grid...  49.5 us
    unnamed x1, local copies, waits for them, and re-layouts  2.09 us

profile of v1, /device:TPU:28, one launch (start us, length us, event | category | flops | bytes accessed | tf_op | source)
XLA Modules:
  0.0 51.6 jit_solution(10457950571063536518)
XLA Ops:
  0.0 49.5 %delta_layer.1 = bf16[192,2048]{1,0:T(8,128)(2,1)} custom-call(bf16[192,1024]{1,0:T(8,128)(2,1)} %q_ref.1, bf16[192,1024]{1,0:T(8,128)(2,1)} %k_ref.1, bf16[192,2048]{1,0:T(8,128)(2,1)} %v_ref.1, bf16[192,1024]{1,0:T(8,128)(2,1)} %q_ref.1, bf16[192,1024]{1,0:T(8,128)(2,1)} %k_ref.1, bf16[192,2048]{1,0:T(8,128)(2,1)} %v_ref.1, f32[16,192]{1,0:T(8,128)} %bitcast.3, ...), custom_call_target="tpu_custom_call" | custom-call | tf_op jit(solution)/shard_map/delta_layer/pallas_call | solution.py:296
  49.6 2.1 %copy.12 = bf16[192,2048]{1,0:T(8,128)(2,1)} copy(bf16[192,2048]{1,0:T(8,128)(2,1)} %delta_layer.1) | data formatting | bytes 1572864

commit v2 on v1

--- a/solution.py
+++ b/solution.py
@@ -10,6 +10,7 @@
 DK = 128
 TILE = 16
 KEY_HEADS_A_STEP = 2
+BLOCK = 64
 F32 = jnp.float32
 BF16 = jnp.bfloat16
 NN = (((1,), (0,)), ((), ()))
@@ -168,8 +169,37 @@
         beta.append(b)
         fade.append(f)
         lower.append(b * grams[r // ratio] * f)
-    inverse = [identity - jnp.where(apart == 1, lower[r], 0.0) for r in heads]
+    blocks = count // BLOCK
+    row_p = lax.broadcasted_iota(jnp.int32, (BLOCK, count), 0)
+    lane_p = lax.broadcasted_iota(jnp.int32, (BLOCK, count), 1)
+    apart_p = jnp.where(row_p >= lane_p % BLOCK, row_p ^ (lane_p % BLOCK), 0)
+    eye_p = (row_p == lane_p % BLOCK).astype(F32)
+    same_block = row // BLOCK == column // BLOCK
+    keep = same_block.astype(F32).astype(BF16)
+
+    def pack(x):
+        packed = x[0:BLOCK, :]
+        for b in range(1, blocks):
+            packed = jnp.where(lane_p // BLOCK == b, x[b * BLOCK : (b + 1) * BLOCK, :], packed)
+        return packed
+
+    def spread(x):
+        return jnp.concatenate([x] * blocks, axis=0) * keep
+
+    lower_p = [pack(lower[r]) for r in heads]
+    inverse = [eye_p - jnp.where(apart_p == 1, lower_p[r], 0.0) for r in heads]
     width = 2
+    while width < BLOCK:
+        mask = (apart_p >= width) & (apart_p < 2 * width)
+        low = [inverse[r].astype(BF16) for r in heads]
+        inner = [
+            dot(jnp.where(mask, lower_p[r], 0.0).astype(BF16), spread(low[r])) for r in heads
+        ]
+        inverse = [inverse[r] - dot(low[r], spread(inner[r].astype(BF16))) for r in heads]
+        width *= 2
+    inverse = [
+        jnp.where(same_block, jnp.concatenate([inverse[r]] * blocks, axis=0), 0.0) for r in heads
+    ]
     while width < count:
         mask = (apart >= width) & (apart < 2 * width)
         low = [inverse[r].astype(BF16) for r in heads]
@@ -187,7 +217,7 @@
             ],
             axis=1,
         )
-        solved.append(dot3(inverse[r], rhs))
+        solved.append(dot2(inverse[r], rhs))
     for r in heads:
         head = step * group + r
         last = cum[r][count - 1 : count, :]
@@ -301,7 +331,7 @@
             col(count, kw), col(count, kw), col(count, vw), whole(beta_t), whole(decay_t),
             col(taps, kw), col(taps, kw), col(taps, vw), whole(gate_proj), whole(gain),
         ],
-        out_specs=whole(gate_proj),
+        out_specs=pl.BlockSpec(memory_space=pltpu.VMEM),
         out_shape=jax.ShapeDtypeStruct(gate_proj.shape, BF16),
         scratch_shapes=[
             pltpu.VMEM((TILE + count, kw), F32),

time: 51.8 us -> 50.7 us (0.979)
  Pallas kernels: 49.5 us -> 48.4 us
    pallas_call x1, Pallas kernels: 49.5 us -> 48.4 us  [shards(): pl.pallas_call(functools.partial(kernel, n, ratio, per_step, steps), grid...]
where the time goes in v2:
time: 50.7 us; the launch traced here: 50.5 us
  Pallas kernels  48.4 us (95%)
  local copies, waits for them, and re-layouts  2.09 us (4%)
    pallas_call x1, Pallas kernels, shards(): pl.pallas_call(functools.partial(kernel, n, ratio, per_step, steps), grid...  48.4 us
    unnamed x1, local copies, waits for them, and re-layouts  2.09 us

profile of v2, /device:TPU:28, one launch (start us, length us, event | category | flops | bytes accessed | tf_op | source)
XLA Modules:
  0.0 50.5 jit_solution(11116636964278566718)
XLA Ops:
  0.0 48.4 %delta_layer.1 = bf16[192,2048]{1,0:T(8,128)(2,1)} custom-call(bf16[192,1024]{1,0:T(8,128)(2,1)} %q_ref.1, bf16[192,1024]{1,0:T(8,128)(2,1)} %k_ref.1, bf16[192,2048]{1,0:T(8,128)(2,1)} %v_ref.1, bf16[192,1024]{1,0:T(8,128)(2,1)} %q_ref.1, bf16[192,1024]{1,0:T(8,128)(2,1)} %k_ref.1, bf16[192,2048]{1,0:T(8,128)(2,1)} %v_ref.1, f32[16,192]{1,0:T(8,128)} %bitcast.3, ...), custom_call_target="tpu_custom_call" | custom-call | tf_op jit(solution)/shard_map/delta_layer/pallas_call | solution.py:326
  48.4 2.1 %copy.12 = bf16[192,2048]{1,0:T(8,128)(2,1)} copy(bf16[192,2048]{1,0:T(8,128)(2,1)} %delta_layer.1) | data formatting | bytes 1572864

commit v3 on v2

--- a/solution.py
+++ b/solution.py
@@ -86,6 +86,7 @@
     count = q_ref.shape[0]
     group = ratio * per_step
     total_heads = group * steps
+    heads = range(group)
     row = lax.broadcasted_iota(jnp.int32, (count, count), 0)
     column = lax.broadcasted_iota(jnp.int32, (count, count), 1)
     upto = row >= column
@@ -145,6 +146,41 @@
 
     def rim_of(ref, w):
         return ref[:, pl.ds(pl.multiple_of(step * w, 128), w)]
+
+    def step_state(h):
+        state = entering[h]
+        new = dot(map_high[h], state) + dot(map_low[h], state) + base_ref[h, 0:DK, :]
+        leaving[h] = new.astype(BF16)
+
+    def forward(p):
+        @pl.when(has_left)
+        def _():
+            for r in heads:
+                hop(p * group + r).wait_recv()
+
+        @pl.when(has_right)
+        def _():
+            for r in heads:
+                step_state(p * group + r)
+            for r in heads:
+                hop(p * group + r).start()
+
+    def forward_each(p):
+        for r in heads:
+            h = p * group + r
+
+            @pl.when(has_left)
+            def _():
+                hop(h).wait_recv()
+
+            @pl.when(has_right)
+            def _():
+                step_state(h)
+                hop(h).start()
+
+    lag = (me + 1) // 2
+    odd = me % 2 == 1
+    ready = step >= lag
 
     kw = per_step * DK
     vw = group * DK
@@ -155,7 +191,6 @@
     keys = [unit(key_all[:, g * DK : (g + 1) * DK]) for g in range(per_step)]
     grams = [dot3(keys[g], keys[g], NT) for g in range(per_step)]
     scores = [dot3(queries[g], keys[g], NT) for g in range(per_step)]
-    heads = range(group)
     lane = lax.broadcasted_iota(jnp.int32, beta_ref.shape, 1)
     cum, beta, fade, lower = [], [], [], []
     for r in heads:
@@ -200,6 +235,10 @@
     inverse = [
         jnp.where(same_block, jnp.concatenate([inverse[r]] * blocks, axis=0), 0.0) for r in heads
     ]
+    @pl.when(jnp.logical_and(ready, odd))
+    def _():
+        forward(step - lag)
+
     while width < count:
         mask = (apart >= width) & (apart < 2 * width)
         low = [inverse[r].astype(BF16) for r in heads]
@@ -231,37 +270,6 @@
         map_low[head] = ml
         reader[head] = (grown[r] * queries[r // ratio] - out[:, DK:]).astype(BF16)
 
-    def step_state(h):
-        state = entering[h]
-        new = dot(map_high[h], state) + dot(map_low[h], state) + base_ref[h, 0:DK, :]
-        leaving[h] = new.astype(BF16)
-
-    def forward(p):
-        @pl.when(has_left)
-        def _():
-            for r in heads:
-                hop(p * group + r).wait_recv()
-
-        @pl.when(has_right)
-        def _():
-            for r in heads:
-                step_state(p * group + r)
-            for r in heads:
-                hop(p * group + r).start()
-
-    def forward_each(p):
-        for r in heads:
-            h = p * group + r
-
-            @pl.when(has_left)
-            def _():
-                hop(h).wait_recv()
-
-            @pl.when(has_right)
-            def _():
-                step_state(h)
-                hop(h).start()
-
     gain = gain_ref[...]
 
     def finish(p):
@@ -273,13 +281,13 @@
             gate = gate_ref[:, place].astype(F32)
             out_ref[:, place] = (rows * lax.rsqrt(mean + 1e-06) * gain * silu(gate)).astype(BF16)
 
-    @pl.when(step >= me)
+    @pl.when(jnp.logical_and(ready, jnp.logical_not(odd)))
     def _():
-        forward(step - me)
+        forward(step - lag)
 
     @pl.when(step == steps - 1)
     def _():
-        start = jnp.maximum(steps - me, 0)
+        start = jnp.maximum(steps - lag, 0)
 
         @pl.loop(start, steps)
         def _(p):

time: 50.7 us -> 50.8 us (level)
  no operation moved by 1% of the time
where the time goes in v3:
time: 50.8 us; the launch traced here: 50.6 us
  Pallas kernels  48.5 us (95%)
  local copies, waits for them, and re-layouts  2.09 us (4%)
    pallas_call x1, Pallas kernels, shards(): pl.pallas_call(functools.partial(kernel, n, ratio, per_step, steps), grid...  48.5 us
    unnamed x1, local copies, waits for them, and re-layouts  2.09 us

profile of v3, /device:TPU:28, one launch (start us, length us, event | category | flops | bytes accessed | tf_op | source)
XLA Modules:
  0.0 50.6 jit_solution(13962220456696029134)
XLA Ops:
  0.0 48.5 %delta_layer.1 = bf16[192,2048]{1,0:T(8,128)(2,1)} custom-call(bf16[192,1024]{1,0:T(8,128)(2,1)} %q_ref.1, bf16[192,1024]{1,0:T(8,128)(2,1)} %k_ref.1, bf16[192,2048]{1,0:T(8,128)(2,1)} %v_ref.1, bf16[192,1024]{1,0:T(8,128)(2,1)} %q_ref.1, bf16[192,1024]{1,0:T(8,128)(2,1)} %k_ref.1, bf16[192,2048]{1,0:T(8,128)(2,1)} %v_ref.1, f32[16,192]{1,0:T(8,128)} %bitcast.3, ...), custom_call_target="tpu_custom_call" | custom-call | tf_op jit(solution)/shard_map/delta_layer/pallas_call | solution.py:334
  48.5 2.1 %copy.12 = bf16[192,2048]{1,0:T(8,128)(2,1)} copy(bf16[192,2048]{1,0:T(8,128)(2,1)} %delta_layer.1) | data formatting | bytes 1572864

commit v4 on v3

--- a/solution.py
+++ b/solution.py
@@ -75,7 +75,8 @@
     out_ref,
     rows_q, rows_k, rows_v, cum_ref, cum_t_ref, beta_ref,
     map_high, map_low, reader, base_ref, rim_q, rim_k, rim_v, entering, leaving,
-    send_sem, recv_sem, rim_send, rim_recv,
+    mate_maps, mate_bases, own, send_sem, recv_sem, map_send, map_recv, base_send, base_recv,
+    rim_send, rim_recv,
 ):
     step = pl.program_id(0)
     me = lax.axis_index("seq")
@@ -100,12 +101,29 @@
             device_id={"seq": right}, device_id_type=pl.DeviceIdType.MESH,
         )
 
-    def hop(h):
+    pair = me // 2
+    second = me % 2 == 1
+    first = jnp.logical_not(second)
+    later = pair > 0
+
+    def hop(source, target, h, sends, receives, device):
         return pltpu.make_async_remote_copy(
-            src_ref=leaving.at[h], dst_ref=entering.at[h],
-            send_sem=send_sem.at[h], recv_sem=recv_sem.at[h],
-            device_id={"seq": right}, device_id_type=pl.DeviceIdType.MESH,
+            src_ref=source.at[h], dst_ref=target.at[h],
+            send_sem=sends.at[h], recv_sem=receives.at[h],
+            device_id={"seq": device}, device_id_type=pl.DeviceIdType.MESH,
         )
+
+    def mate_map(h):
+        return hop(map_high, mate_maps, h, map_send, map_recv, right)
+
+    def mate_base(h):
+        return hop(leaving, mate_bases, h, base_send, base_recv, right)
+
+    def to_first(h):
+        return hop(leaving, entering, h, base_send, recv_sem, right)
+
+    def to_second(h):
+        return hop(leaving, entering, h, send_sem, recv_sem, lax.rem(me + 2, n))
 
     @pl.when(step == 0)
     def _():
@@ -117,9 +135,23 @@
                 barrier, inc=1, device_id={"seq": left}, device_id_type=pl.DeviceIdType.MESH
             )
 
+        @pl.when(jnp.logical_and(second, later))
+        def _():
+            pl.semaphore_signal(
+                barrier, inc=1, device_id={"seq": lax.rem(me + n - 2, n)},
+                device_id_type=pl.DeviceIdType.MESH,
+            )
+
+        @pl.when(jnp.logical_and(second, has_right))
+        def _():
+            pl.semaphore_wait(barrier, 2)
+
+        @pl.when(first)
+        def _():
+            pl.semaphore_wait(barrier, 1)
+
         @pl.when(has_right)
         def _():
-            pl.semaphore_wait(barrier, 1)
             for i in range(3):
                 rim_hop(i).start()
 
@@ -128,9 +160,12 @@
         cum_t_ref[...] = precise(decay_t[...], ones, NT)
         beta_ref[...] = precise(identity, beta_t[...], NT)
 
+        @pl.when(jnp.logical_not(later))
+        def _():
+            entering[...] = jnp.zeros_like(entering)
+
         @pl.when(jnp.logical_not(has_left))
         def _():
-            entering[...] = jnp.zeros_like(entering)
             for ref in (rim_q, rim_k, rim_v):
                 ref[...] = jnp.zeros_like(ref)
 
@@ -147,40 +182,63 @@
     def rim_of(ref, w):
         return ref[:, pl.ds(pl.multiple_of(step * w, 128), w)]
 
+    def await_state(h):
+        @pl.when(later)
+        def _():
+            to_second(h).wait_recv()
+
+        @pl.when(second)
+        def _():
+            mate_base(h).wait_recv()
+            mate_map(h).wait_recv()
+
+    def own_state(h):
+        state = dot(mate_maps[h, 0:DK], entering[h]) + mate_bases[h].astype(F32)
+        own[h] = state.astype(BF16)
+
     def step_state(h):
-        state = entering[h]
+        state = own[h]
         new = dot(map_high[h], state) + dot(map_low[h], state) + base_ref[h, 0:DK, :]
         leaving[h] = new.astype(BF16)
 
+    def send_state(h):
+        to_second(h).start()
+        to_first(h).start()
+
     def forward(p):
-        @pl.when(has_left)
-        def _():
-            for r in heads:
-                hop(p * group + r).wait_recv()
+        for r in heads:
+            await_state(p * group + r)
+        for r in heads:
+            own_state(p * group + r)
 
         @pl.when(has_right)
         def _():
             for r in heads:
                 step_state(p * group + r)
             for r in heads:
-                hop(p * group + r).start()
+                send_state(p * group + r)
 
     def forward_each(p):
         for r in heads:
             h = p * group + r
-
-            @pl.when(has_left)
+            await_state(h)
+
+            @pl.when(first)
             def _():
-                hop(h).wait_recv()
-
-            @pl.when(has_right)
+                own[h] = entering[h]
+
+            @pl.when(second)
             def _():
-                step_state(h)
-                hop(h).start()
-
-    lag = (me + 1) // 2
-    odd = me % 2 == 1
-    ready = step >= lag
+                own_state(h)
+
+                @pl.when(has_right)
+                def _():
+                    step_state(h)
+                    send_state(h)
+
+    lag = 1 + (pair + 1) // 2
+    odd = pair % 2 == 1
+    ready = jnp.logical_and(second, step >= lag)
 
     kw = per_step * DK
     vw = group * DK
@@ -276,18 +334,27 @@
         for r in heads:
             h = p * group + r
             place = pl.ds(pl.multiple_of(h * DK, DK), DK)
-            rows = dot(reader[h], entering[h]) + base_ref[h, DK : DK + count, :]
+            rows = dot(reader[h], own[h]) + base_ref[h, DK : DK + count, :]
             mean = jnp.mean(rows * rows, axis=-1, keepdims=True)
             gate = gate_ref[:, place].astype(F32)
             out_ref[:, place] = (rows * lax.rsqrt(mean + 1e-06) * gain * silu(gate)).astype(BF16)
 
+    @pl.when(first)
+    def _():
+        for r in heads:
+            head = step * group + r
+            leaving[head] = base_ref[head, 0:DK, :].astype(BF16)
+            mate_base(head).start()
+        for r in heads:
+            mate_map(step * group + r).start()
+
     @pl.when(jnp.logical_and(ready, jnp.logical_not(odd)))
     def _():
         forward(step - lag)
 
     @pl.when(step == steps - 1)
     def _():
-        start = jnp.maximum(steps - lag, 0)
+        start = jnp.where(second, jnp.maximum(steps - lag, 0), 0)
 
         @pl.loop(start, steps)
         def _(p):
@@ -298,10 +365,17 @@
         def _(p):
             finish(p)
 
-        @pl.when(has_right)
-        def _():
-            for h in range(total_heads):
-                hop(h).wait_send()
+        @pl.loop(0, total_heads)
+        def _(h):
+            @pl.when(first)
+            def _():
+                mate_base(h).wait_send()
+                mate_map(h).wait_send()
+
+            @pl.when(jnp.logical_and(second, has_right))
+            def _():
+                to_first(h).wait_send()
+                to_second(h).wait_send()
 
 
 def shards(
@@ -357,6 +431,13 @@
             pltpu.VMEM((TILE, value_proj.shape[1]), BF16),
             pltpu.VMEM((heads, DK, DK), BF16),
             pltpu.VMEM((heads, DK, DK), BF16),
+            pltpu.VMEM((heads, DK, DK), BF16),
+            pltpu.VMEM((heads, DK, DK), BF16),
+            pltpu.VMEM((heads, DK, DK), BF16),
+            pltpu.SemaphoreType.DMA((heads,)),
+            pltpu.SemaphoreType.DMA((heads,)),
+            pltpu.SemaphoreType.DMA((heads,)),
+            pltpu.SemaphoreType.DMA((heads,)),
             pltpu.SemaphoreType.DMA((heads,)),
             pltpu.SemaphoreType.DMA((heads,)),
             pltpu.SemaphoreType.DMA((3,)),

time: 50.8 us -> 54.5 us (1.073); the launches traced: 50.6 us -> 53.6 us
  Pallas kernels: 48.5 us -> 51.5 us
    pallas_call x1, Pallas kernels: 48.5 us -> 51.5 us  [shards(): pl.pallas_call(functools.partial(kernel, n, ratio, per_step, steps), grid...]
where the time goes in v4:
time: 54.5 us; the launch traced here: 53.6 us
  Pallas kernels  51.5 us (94%)
  local copies, waits for them, and re-layouts  2.09 us (4%)
    pallas_call x1, Pallas kernels, shards(): pl.pallas_call(functools.partial(kernel, n, ratio, per_step, steps), grid...  51.5 us
    unnamed x1, local copies, waits for them, and re-layouts  2.09 us

profile of v4, /device:TPU:28, one launch (start us, length us, event | category | flops | bytes accessed | tf_op | source)
XLA Modules:
  0.0 53.6 jit_solution(17461397588232154870)
XLA Ops:
  0.0 51.5 %delta_layer.1 = bf16[192,2048]{1,0:T(8,128)(2,1)} custom-call(bf16[192,1024]{1,0:T(8,128)(2,1)} %q_ref.1, bf16[192,1024]{1,0:T(8,128)(2,1)} %k_ref.1, bf16[192,2048]{1,0:T(8,128)(2,1)} %v_ref.1, bf16[192,1024]{1,0:T(8,128)(2,1)} %q_ref.1, bf16[192,1024]{1,0:T(8,128)(2,1)} %k_ref.1, bf16[192,2048]{1,0:T(8,128)(2,1)} %v_ref.1, f32[16,192]{1,0:T(8,128)} %bitcast.3, ...), custom_call_target="tpu_custom_call" | custom-call | tf_op jit(solution)/shard_map/delta_layer/pallas_call | solution.py:408
  51.5 2.1 %copy.12 = bf16[192,2048]{1,0:T(8,128)(2,1)} copy(bf16[192,2048]{1,0:T(8,128)(2,1)} %delta_layer.1) | data formatting | bytes 1572864

commit v5 on v3

--- a/solution.py
+++ b/solution.py
@@ -9,7 +9,7 @@
 
 DK = 128
 TILE = 16
-KEY_HEADS_A_STEP = 2
+KEY_HEADS_A_STEP = 1
 BLOCK = 64
 F32 = jnp.float32
 BF16 = jnp.bfloat16

time: 50.8 us -> 61.3 us (1.21)
  Pallas kernels: 48.5 us -> 59 us
    pallas_call x1, Pallas kernels: 48.5 us -> 59 us  [shards(): pl.pallas_call(functools.partial(kernel, n, ratio, per_step, steps), grid...]
where the time goes in v5:
time: 61.3 us; the launch traced here: 61.1 us
  Pallas kernels  59 us (96%)
  local copies, waits for them, and re-layouts  2.09 us (3%)
    pallas_call x1, Pallas kernels, shards(): pl.pallas_call(functools.partial(kernel, n, ratio, per_step, steps), grid...  59 us
    unnamed x1, local copies, waits for them, and re-layouts  2.09 us

profile of v5, /device:TPU:28, one launch (start us, length us, event | category | flops | bytes accessed | tf_op | source)
XLA Modules:
  0.0 61.1 jit_solution(5859061260239566664)
XLA Ops:
  0.0 59.0 %delta_layer.1 = bf16[192,2048]{1,0:T(8,128)(2,1)} custom-call(bf16[192,1024]{1,0:T(8,128)(2,1)} %q_ref.1, bf16[192,1024]{1,0:T(8,128)(2,1)} %k_ref.1, bf16[192,2048]{1,0:T(8,128)(2,1)} %v_ref.1, bf16[192,1024]{1,0:T(8,128)(2,1)} %q_ref.1, bf16[192,1024]{1,0:T(8,128)(2,1)} %k_ref.1, bf16[192,2048]{1,0:T(8,128)(2,1)} %v_ref.1, f32[16,192]{1,0:T(8,128)} %bitcast.3, ...), custom_call_target="tpu_custom_call" | custom-call | tf_op jit(solution)/shard_map/delta_layer/pallas_call | solution.py:334
  59.0 2.1 %copy.12 = bf16[192,2048]{1,0:T(8,128)(2,1)} copy(bf16[192,2048]{1,0:T(8,128)(2,1)} %delta_layer.1) | data formatting | bytes 1572864

commit v6 on v5

--- a/solution.py
+++ b/solution.py
@@ -9,7 +9,7 @@
 
 DK = 128
 TILE = 16
-KEY_HEADS_A_STEP = 1
+KEY_HEADS_A_STEP = 4
 BLOCK = 64
 F32 = jnp.float32
 BF16 = jnp.bfloat16

time: 61.3 us -> 52.3 us (0.85)
  Pallas kernels: 59 us -> 50 us
    pallas_call x1, Pallas kernels: 59 us -> 50 us  [shards(): pl.pallas_call(functools.partial(kernel, n, ratio, per_step, steps), grid...]
where the time goes in v6:
time: 52.3 us; the launch traced here: 52.1 us
  Pallas kernels  50 us (96%)
  local copies, waits for them, and re-layouts  2.09 us (4%)
    pallas_call x1, Pallas kernels, shards(): pl.pallas_call(functools.partial(kernel, n, ratio, per_step, steps), grid...  50 us
    unnamed x1, local copies, waits for them, and re-layouts  2.09 us

profile of v6, /device:TPU:28, one launch (start us, length us, event | category | flops | bytes accessed | tf_op | source)
XLA Modules:
  0.0 52.1 jit_solution(8924991812981966569)
XLA Ops:
  0.0 50.0 %delta_layer.1 = bf16[192,2048]{1,0:T(8,128)(2,1)} custom-call(bf16[192,1024]{1,0:T(8,128)(2,1)} %q_ref.1, bf16[192,1024]{1,0:T(8,128)(2,1)} %k_ref.1, bf16[192,2048]{1,0:T(8,128)(2,1)} %v_ref.1, bf16[192,1024]{1,0:T(8,128)(2,1)} %q_ref.1, bf16[192,1024]{1,0:T(8,128)(2,1)} %k_ref.1, bf16[192,2048]{1,0:T(8,128)(2,1)} %v_ref.1, f32[16,192]{1,0:T(8,128)} %bitcast.3, ...), custom_call_target="tpu_custom_call" | custom-call | tf_op jit(solution)/shard_map/delta_layer/pallas_call | solution.py:334
  50.0 2.1 %copy.12 = bf16[192,2048]{1,0:T(8,128)(2,1)} copy(bf16[192,2048]{1,0:T(8,128)(2,1)} %delta_layer.1) | data formatting | bytes 1572864
